TPU v7x, 32 devices: a whole 2x2x4 slice. The times are simulated.
32 devices in a mesh: dp: 8 (over z, x), tensor: 4 (over y, core).
Axes of the slice: x: 2, y: 2, z: 4, core: 2. Of those that a mesh axis runs over, the one named last changes fastest.
Arguments:
- hidden_in: bfloat16 [8192, 1152], P(('dp', 'tensor')), may hold values from -6 to 6
- picture_ids: int32 [8192], P('dp'), may hold values from -1 to 9, as said below
- norm1_gain: float32 [1152], replicated, may hold values from 0.5 to 1.5
- norm1_bias: float32 [1152], replicated, may hold values from -1.75 to 1.75
- w_qkv: bfloat16 [3, 1152, 1152], P(None, None, 'tensor'), may hold values from -1 to 1
- qv_bias: float32 [2, 1152], P(None, 'tensor'), may hold values from -3 to 3
- w_out: bfloat16 [1152, 1152], P('tensor'), may hold values from -0.75 to 0.75
- out_bias: float32 [1152], replicated, may hold values from -1.75 to 1.75
- norm2_gain: float32 [1152], replicated, may hold values from 0.5 to 1.5
- norm2_bias: float32 [1152], replicated, may hold values from -1.75 to 1.75
- w_up: bfloat16 [1152, 4304], P(None, 'tensor'), may hold values from -0.1875 to 0.1875
- up_bias: float32 [4304], P('tensor'), may hold values from -3 to 3
- w_down: bfloat16 [4304, 1152], P('tensor'), may hold values from -0.125 to 0.125
- down_bias: float32 [1152], replicated, may hold values from -1.75 to 1.75
- cotangent: bfloat16 [8192, 1152], P(('dp', 'tensor')), may hold values from -6 to 6
Outputs:
- hidden_out: bfloat16 [8192, 1152], P(('dp', 'tensor'))
- grad_in: bfloat16 [8192, 1152], P(('dp', 'tensor'))
- grad_qkv: float32 [3, 1152, 1152], P(None, 'dp', 'tensor')
- grad_out: float32 [1152, 1152], P('tensor', 'dp')
- grad_up: float32 [1152, 4304], P('dp', 'tensor')
- grad_down: float32 [4304, 1152], P('tensor', 'dp')
- grad_qv_bias: float32 [2, 1152], P(None, 'tensor')
- grad_up_bias: float32 [4304], P('tensor')
- grad_shared: float32 [6, 1152], replicated
- head_maxima: float32 [16], P('tensor')
- scaled_qk: bfloat16 [2, 1152, 1152], P(None, None, 'tensor')
- scaled_query_bias: float32 [1152], P('tensor')
Inputs may be any that keep to these rules, and one draw needn't show every extreme that they name: `picture_ids`: each aligned row of 1024 tokens holds whole pictures of 100 to 1024 patches one after another, numbered from 0 within the row, then padding with id -1; some row holds a single picture of 1024 patches, and some other row holds 10 pictures of 100 patches.
All inputs are finite; a program needn't handle non-finite values.
Results may differ from a plain program's by a relative error of at most 0.014.
Values may be sent and summed in bfloat16 or wider, within the bound.
No kernel may reach another device: no remote copies, remote signals or barrier semaphores. Data moves between devices by JAX's collectives and lax.ppermute only.
A program may use at most 192 MiB of HBM per device.

v0:
```python
import jax
import jax.numpy as jnp
from jax import lax
from jax.sharding import PartitionSpec as P

HEAD_DIM = 72
PACK = 1024
QBLOCK = 512
CLIP_LIMIT = 9
eps_norm = 1e-06
neg_fill = -1e30


def normalize(values_in, gain, shift):
    row_mean = jnp.mean(values_in, axis=-1, keepdims=True)
    centred = values_in - row_mean
    variance = jnp.mean(centred * centred, axis=-1, keepdims=True)
    inverse = lax.rsqrt(variance + eps_norm)
    unit_rows = centred * inverse
    return (unit_rows * gain + shift, unit_rows, inverse)


def norm_back(grad_rows, unit_rows, inverse, gain):
    scaled = grad_rows * gain
    return inverse * (
        scaled
        - jnp.mean(scaled, axis=-1, keepdims=True)
        - unit_rows * jnp.mean(scaled * unit_rows, axis=-1, keepdims=True)
    )


def gelu_tanh(inputs):
    return jax.nn.gelu(inputs, approximate=True)


def local(
    hidden_in,
    picture_ids,
    norm1_gain,
    norm1_bias,
    w_qkv,
    qv_bias,
    w_out,
    out_bias,
    norm2_gain,
    norm2_bias,
    w_up,
    up_bias,
    w_down,
    down_bias,
    cotangent,
):
    group_rows = picture_ids.shape[0]
    row_count = group_rows // PACK
    head_width = w_qkv.shape[2]
    local_heads = head_width // HEAD_DIM
    score_scale = HEAD_DIM ** (-0.5)
    block_count = PACK // QBLOCK
    block_shape = (row_count, block_count, QBLOCK, local_heads, HEAD_DIM)
    row_shape = (row_count, PACK, local_heads, HEAD_DIM)
    source = hidden_in.astype(jnp.float32)
    normed_a, unit_a, inverse_a = normalize(source, norm1_gain, norm1_bias)
    whole_a = lax.all_gather(normed_a.astype(jnp.bfloat16), "tensor", axis=0, tiled=True)
    projected = jnp.einsum("td,cde->cte", whole_a, w_qkv, preferred_element_type=jnp.float32)
    queries = (projected[0] + qv_bias[0]).astype(jnp.bfloat16)
    key_rows = projected[1].astype(jnp.bfloat16)
    values = (projected[2] + qv_bias[1]).astype(jnp.bfloat16)
    query_blocks = queries.reshape(block_shape)
    key_heads = key_rows.reshape(row_shape)
    value_heads = values.reshape(row_shape)
    row_ids = picture_ids.reshape(row_count, PACK)

    def attend_row(parts_in):
        row_q, row_k, row_v, ids_row = parts_in
        block_ids = ids_row.reshape(block_count, QBLOCK)

        def attend_block(block_in):
            block_q, query_ids = block_in
            scores = (
                jnp.einsum("qhd,khd->hqk", block_q, row_k, preferred_element_type=jnp.float32)
                * score_scale
            )
            allowed = query_ids[:, None] == ids_row[None, :]
            scores = jnp.where(allowed[None], scores, neg_fill)
            row_top = jnp.max(scores, axis=2, keepdims=True)
            weights = jnp.exp(scores - row_top)
            row_sum = jnp.sum(weights, axis=2, keepdims=True)
            prob_rows = (weights / row_sum).astype(jnp.bfloat16)
            attended = jnp.einsum(
                "hqk,khd->qhd", prob_rows, row_v, preferred_element_type=jnp.float32
            )
            return (
                attended.astype(jnp.bfloat16),
                (row_top + jnp.log(row_sum))[:, :, 0],
                jnp.max(row_top[:, :, 0], axis=1),
            )

        return lax.map(attend_block, (row_q, block_ids))

    attended, log_total, block_top = lax.map(
        attend_row, (query_blocks, key_heads, value_heads, row_ids)
    )
    flat_att = attended.reshape(group_rows, head_width)
    branch_a = lax.psum_scatter(
        jnp.dot(flat_att, w_out, preferred_element_type=jnp.float32),
        "tensor",
        scatter_dimension=0,
        tiled=True,
    )
    residual = source + branch_a + out_bias
    normed_b, unit_b, inverse_b = normalize(residual, norm2_gain, norm2_bias)
    whole_b = lax.all_gather(normed_b.astype(jnp.bfloat16), "tensor", axis=0, tiled=True)
    pre_act = jnp.dot(whole_b, w_up, preferred_element_type=jnp.float32) + up_bias
    activated = gelu_tanh(pre_act).astype(jnp.bfloat16)
    branch_b = lax.psum_scatter(
        jnp.dot(activated, w_down, preferred_element_type=jnp.float32).astype(jnp.bfloat16),
        "tensor",
        scatter_dimension=0,
        tiled=True,
    ).astype(jnp.float32)
    hidden_out = (residual + branch_b + down_bias).astype(jnp.bfloat16)
    head_maxima = lax.pmax(jnp.max(block_top, axis=(0, 1)), "dp")
    limit = jnp.float32(CLIP_LIMIT)
    factor = jnp.sqrt(limit / jnp.maximum(head_maxima, limit))
    column = jnp.repeat(factor, HEAD_DIM)
    scaled_qk = (w_qkv[:2].astype(jnp.float32) * column).astype(jnp.bfloat16)
    scaled_query_bias = qv_bias[0] * column
    whole_grad = lax.all_gather(cotangent, "tensor", axis=0, tiled=True)
    grad_act = jnp.einsum("td,fd->tf", whole_grad, w_down, preferred_element_type=jnp.float32)
    grad_pre = jax.vjp(gelu_tanh, pre_act)[1](grad_act)[0].astype(jnp.bfloat16)
    grad_down = jnp.einsum("tf,td->fd", activated, whole_grad, preferred_element_type=jnp.float32)
    grad_up = jnp.einsum("td,tf->df", whole_b, grad_pre, preferred_element_type=jnp.float32)
    grad_up_bias = jnp.sum(grad_pre, axis=0, dtype=jnp.float32)
    grad_norm_b = lax.psum_scatter(
        jnp.einsum("tf,df->td", grad_pre, w_up, preferred_element_type=jnp.float32),
        "tensor",
        scatter_dimension=0,
        tiled=True,
    )
    grad_top = cotangent.astype(jnp.float32)
    grad_resid = grad_top + norm_back(grad_norm_b, unit_b, inverse_b, norm2_gain)
    grad_branch = grad_resid.astype(jnp.bfloat16)
    whole_branch = lax.all_gather(grad_branch, "tensor", axis=0, tiled=True)
    grad_out = jnp.einsum("te,td->ed", flat_att, whole_branch, preferred_element_type=jnp.float32)
    grad_att = jnp.einsum(
        "td,ed->te", whole_branch, w_out, preferred_element_type=jnp.float32
    ).astype(jnp.bfloat16)

    def back_row(parts_in):
        row_q, row_k, row_v, ids_row, row_grad, row_lse = parts_in
        block_ids = ids_row.reshape(block_count, QBLOCK)

        def back_block(state_in, block_in):
            key_grad, value_grad = state_in
            block_q, query_ids, block_grad, block_lse = block_in
            scores = (
                jnp.einsum("qhd,khd->hqk", block_q, row_k, preferred_element_type=jnp.float32)
                * score_scale
            )
            allowed = query_ids[:, None] == ids_row[None, :]
            scores = jnp.where(allowed[None], scores, neg_fill)
            prob_full = jnp.exp(scores - block_lse[:, :, None])
            grad_probs = jnp.einsum(
                "qhd,khd->hqk", block_grad, row_v, preferred_element_type=jnp.float32
            )
            inner = jnp.sum(prob_full * grad_probs, axis=2, keepdims=True)
            grad_scores = (prob_full * (grad_probs - inner)).astype(jnp.bfloat16)
            query_grad = (
                jnp.einsum("hqk,khd->qhd", grad_scores, row_k, preferred_element_type=jnp.float32)
                * score_scale
            )
            key_grad = (
                key_grad
                + jnp.einsum(
                    "hqk,qhd->khd", grad_scores, block_q, preferred_element_type=jnp.float32
                )
                * score_scale
            )
            value_grad = value_grad + jnp.einsum(
                "hqk,qhd->khd",
                prob_full.astype(jnp.bfloat16),
                block_grad,
                preferred_element_type=jnp.float32,
            )
            return ((key_grad, value_grad), query_grad.astype(jnp.bfloat16))

        zero_rows = jnp.zeros(row_k.shape, jnp.float32)
        (key_grad, value_grad), query_grad = lax.scan(
            back_block, (zero_rows, zero_rows), (row_q, block_ids, row_grad, row_lse)
        )
        return (query_grad, key_grad.astype(jnp.bfloat16), value_grad.astype(jnp.bfloat16))

    query_grad, key_grad, value_grad = lax.map(
        back_row,
        (query_blocks, key_heads, value_heads, row_ids, grad_att.reshape(block_shape), log_total),
    )
    grad_stack = jnp.stack(
        [
            query_grad.reshape(group_rows, head_width),
            key_grad.reshape(group_rows, head_width),
            value_grad.reshape(group_rows, head_width),
        ]
    )
    grad_qkv = jnp.einsum("td,cte->cde", whole_a, grad_stack, preferred_element_type=jnp.float32)
    grad_qv_bias = jnp.stack(
        [
            jnp.sum(grad_stack[0], axis=0, dtype=jnp.float32),
            jnp.sum(grad_stack[2], axis=0, dtype=jnp.float32),
        ]
    )
    grad_norm_a = lax.psum_scatter(
        jnp.einsum("cte,cde->td", grad_stack, w_qkv, preferred_element_type=jnp.float32),
        "tensor",
        scatter_dimension=0,
        tiled=True,
    )
    grad_in = (grad_resid + norm_back(grad_norm_a, unit_a, inverse_a, norm1_gain)).astype(
        jnp.bfloat16
    )
    grad_qkv, grad_out, grad_up, grad_down = (
        lax.psum_scatter(grad_qkv, "dp", scatter_dimension=1, tiled=True),
        lax.psum_scatter(grad_out, "dp", scatter_dimension=1, tiled=True),
        lax.psum_scatter(grad_up, "dp", scatter_dimension=0, tiled=True),
        lax.psum_scatter(grad_down, "dp", scatter_dimension=1, tiled=True),
    )
    grad_qv_bias, grad_up_bias = lax.psum((grad_qv_bias, grad_up_bias), "dp")
    shared_part = jnp.stack(
        [
            jnp.sum(grad_norm_a * unit_a, axis=0),
            jnp.sum(grad_norm_a, axis=0),
            jnp.sum(grad_resid, axis=0),
            jnp.sum(grad_norm_b * unit_b, axis=0),
            jnp.sum(grad_norm_b, axis=0),
            jnp.sum(grad_top, axis=0),
        ]
    )
    grad_shared = lax.psum(shared_part, ("dp", "tensor"))
    return (
        hidden_out,
        grad_in,
        grad_qkv,
        grad_out,
        grad_up,
        grad_down,
        grad_qv_bias,
        grad_up_bias,
        grad_shared,
        head_maxima,
        scaled_qk,
        scaled_query_bias,
    )


def solution(mesh):
    return jax.shard_map(
        local,
        mesh=mesh,
        in_specs=(
            P(("dp", "tensor"), None),
            P("dp"),
            P(),
            P(),
            P(None, None, "tensor"),
            P(None, "tensor"),
            P("tensor", None),
            P(),
            P(),
            P(),
            P(None, "tensor"),
            P("tensor"),
            P("tensor", None),
            P(),
            P(("dp", "tensor"), None),
        ),
        out_specs=(
            P(("dp", "tensor"), None),
            P(("dp", "tensor"), None),
            P(None, "dp", "tensor"),
            P("tensor", "dp"),
            P("dp", "tensor"),
            P("tensor", "dp"),
            P(None, "tensor"),
            P("tensor"),
            P(),
            P("tensor"),
            P(None, None, "tensor"),
            P("tensor"),
        ),
        check_vma=False,
    )
```

profile of v0, /device:TPU:0, one launch (start us, length us, event | category | flops | bytes accessed | tf_op | source)
XLA Modules:
  0.0 802.8 jit_solution(1162977882640721757)
XLA Ops:
  7.3 1.4 convert_reduce_fusion.1
  8.6 1.4 fusion.71
  10.0 2.2 fusion.64
  12.5 26.6 %all-gather.5.cloned.1.call-done = bf16[1024,1152]{1,0:T(8,128)(2,1)} async-done(((bf16[256,1152]{1,0:T(8,128)(2,1)}), bf16[1024,1152]{1,0:T(8,128)(2,1)}) %all-gather.5.cloned.1.call-update) | async-done | bytes 2359312 | tf_op jit(solution)/shard_map/all_gather | solution.py:63
  39.2 4.7 fusion.54
  44.0 1.6 fusion.81
  45.6 3.2 squeeze.52
  48.8 2.3 add_convert_fusion.2
  53.0 20.3 %while.51 = (s32[]{:T(128)}, bf16[2,512,4,72]{1,3,2,0:T(8,128)(2,1)}, f32[2,4,512]{2,1,0:T(4,128)S(1)}, f32[2,4]{1,0:T(2,128)S(1)}, s32[2,512]{1,0:T(2,128)S(1)}...) while((s32[]{:T(128)}, ...), condition=%wide.region_6.7_spmd, body=%wide.region_2.6_spmd.sunk | while | flops 631912448 | bytes 36186380 | solution.py:98
  53.4 2.8 fusion.132
  56.2 2.9 fusion.133
  59.2 3.1 fusion.134
  63.6 2.8 fusion.132
  66.4 2.9 fusion.133
  69.3 3.1 fusion.134
  73.4 1.7 copy.37
  76.0 3.6 fusion.82
  80.5 47.2 %reduce-scatter.11.cloned.1.call-done = f32[256,1152]{1,0:T(8,128)} async-done(((f32[1024,1152]{1,0:T(8,128)}), f32[256,1152]{1,0:T(8,128)}) %reduce-scatter.11.cloned.1.call-update) | async-done | bytes 1179664 | tf_op jit(solution)/shard_map/reduce_scatter | solution.py:104
  127.7 1.7 fusion.79
  131.7 21.7 %all-gather.9.cloned.1.call-done = bf16[1024,1152]{1,0:T(8,128)(2,1)} async-done(((bf16[256,1152]{1,0:T(8,128)(2,1)}), bf16[1024,1152]{1,0:T(8,128)(2,1)}) %all-gather.9.cloned.1.call-update) | async-done | bytes 2359312 | tf_op jit(solution)/shard_map/all_gather | solution.py:128
  153.5 7.5 fusion.83
  161.0 18.6 %all-gather.7.cloned.1.call-done = bf16[1024,1152]{1,0:T(8,128)(2,1)} async-done(((bf16[256,1152]{1,0:T(8,128)(2,1)}), bf16[1024,1152]{1,0:T(8,128)(2,1)}) %all-gather.7.cloned.1.call-update) | async-done | bytes 2359312 | tf_op jit(solution)/shard_map/all_gather | solution.py:112
  179.6 9.9 %convert_reduce_fusion = (f32[1076]{0:T(1024)}, bf16[1024,1076]{0,1:T(8,128)(2,1)S(1)}, f32[1024,1076]{0,1:T(8,128)}) fusion(f32[1024,1076]{0,1:T(8,128)} %fusion.83, f32[1076]{0:T(1024)S(1)} %copy-done.48, bf16[1024,1152]{1,0:T(8,128)(2,1)} %all-gather.7.cloned.1.call-done, bf16[1152,1076]{0,1:T(8,128)(2,1)S(1)} %copy-done), kind=kOutput, calls=%fused_computation.63 | convolution fusion | flops 2563943424 | bytes 15865248 | tf_op jit(solution)/shard_map/dot_general | solution.py:113
  189.5 1.4 copy-done.50
  190.9 5.2 fusion.84
  196.2 1.6 copy-done.47
  197.8 7.5 convolution_convert_fusion
  205.4 38.8 %reduce-scatter.15.cloned.1.call-done = f32[256,1152]{1,0:T(8,128)} async-done(((f32[1024,1152]{1,0:T(8,128)}), f32[256,1152]{1,0:T(8,128)}) %reduce-scatter.15.cloned.1.call-update) | async-done | bytes 1179664 | tf_op jit(solution)/shard_map/reduce_scatter | solution.py:134
  244.1 2.4 multiply_reduce_fusion.1
  246.5 33.1 %reduce-scatter.13.cloned.1.call-done = bf16[256,1152]{1,0:T(8,128)(2,1)} async-done(((bf16[1024,1152]{1,0:T(8,128)(2,1)}), bf16[256,1152]{1,0:T(8,128)(2,1)}) %reduce-scatter.13.cloned.1.call-update) | async-done | bytes 589840 | tf_op jit(solution)/shard_map/reduce_scatter | solution.py:115
  279.6 3.6 fusion.77
  284.5 23.9 %all-gather.11.cloned.1.call-done = bf16[1024,1152]{1,0:T(8,128)(2,1)} async-done(((bf16[256,1152]{1,0:T(8,128)(2,1)}), bf16[1024,1152]{1,0:T(8,128)(2,1)}) %all-gather.11.cloned.1.call-update) | async-done | bytes 2359312 | tf_op jit(solution)/shard_map/all_gather | solution.py:143
  308.4 3.6 convolution_convert_fusion.1
  312.0 2.3 squeeze.54
  316.0 25.9 %while.52 = (s32[]{:T(128)}, f32[1024,4,72]{0,2,1:T(8,128)S(1)}, f32[1024,4,72]{0,2,1:T(8,128)}, bf16[2,512,4,72]{1,3,2,0:T(8,128)(2,1)}, bf16[2,512,4,72]{1,3,2...) while((s32[]{:T(128)}, f32[1024,4,72]{0,2,1:T(8,128)S(1)}, ...), condition=%wide.region_16.17_spmd.clone, body=%wide.region_14.16_spmd.clone.sunk | while | flops 1543698432 | bytes 91916632 | solution.py:188
  317.8 2.6 fusion.146
  320.5 3.3 multiply_reduce_fusion.7
  323.8 2.4 multiply_convert_fusion.6
  326.3 1.4 fusion.147
  330.6 2.6 fusion.146
  333.3 3.3 multiply_reduce_fusion.7
  336.6 2.4 multiply_convert_fusion.6
  339.0 1.4 fusion.147
  342.0 1.9 copy.39
  344.6 6.3 convolution_bitcast_fusion.1
  350.9 8.6 %copy.41 = f32[3,1152,288]{2,0,1:T(4,128)} copy(f32[3,1152,288]{1,2,0:T(8,128)} %convolution_bitcast_fusion.1) | data formatting | bytes 7962624
  359.5 9.0 %reshape.211 = f32[1152,864]{1,0:T(8,128)} reshape(f32[1152,3,288]{2,1,0:T(4,128)} %bitcast.143) | data formatting | bytes 7962624
  368.5 1.5 copy-done.21
  370.1 6.3 convolution_bitcast_fusion
  376.5 8.6 %fusion.76 = f32[1076,1152]{0,1:T(8,128)} fusion(bf16[1024,1152]{1,0:T(8,128)(2,1)} %all-gather.9.cloned.1.call-done, f32[1024,1076]{0,1:T(8,128)} %get-tuple-element.355), kind=kOutput, calls=%fused_computation.124 | convolution fusion | flops 2548518912 | bytes 11724800 | tf_op jit(solution)/shard_map/tf,td->fd/dot_general | solution.py:131
  385.4 8.0 fusion.86
  394.5 4.4 fusion.85
  399.1 22.0 %pmax.7 = f32[4]{0:T(128)S(1)} all-reduce(f32[4]{0:T(128)S(1)} %reduce_max.27), channel_id=1, replica_groups=mesh['dp'=8,'tensor'=4] {'dp'}, use_global_device_ids=true, to_apply=%region_37.38 | all-reduce | flops 4 | bytes 32 | tf_op jit(solution)/shard_map/pmax | solution.py:122
  421.8 1.3 multiply_convert_fusion.2
  423.7 34.2 %all-reduce = (f32[2,288]{1,0:T(2,128)}, f32[1076]{0:T(1024)}) all-reduce(f32[2,288]{1,0:T(2,128)S(1)} %pad_maximum_fusion.3, f32[1076]{0:T(1024)S(1)} %copy-done.43), channel_id=1, replica_groups=mesh['dp'=8,'tensor'=4] {'dp'}, use_global_device_ids=true, to_apply=%region_26.27 | all-reduce | flops 1652 | bytes 13216 | tf_op jit(solution)/shard_map/psum | solution.py:226
  457.9 2.4 reshape.212
  460.3 2.2 copy.40
  462.5 44.9 %reduce-scatter.17.cloned.1.call-done = f32[256,1152]{1,0:T(8,128)} async-done(((f32[1024,1152]{1,0:T(8,128)}), f32[256,1152]{1,0:T(8,128)}) %reduce-scatter.17.cloned.1.call-update) | async-done | bytes 1179664 | tf_op jit(solution)/shard_map/reduce_scatter | solution.py:211
  507.4 1.9 fusion.70
  509.3 42.9 %psum.23 = f32[6,1152]{1,0:T(8,128)} all-reduce(f32[6,1152]{1,0:T(8,128)S(1)} %stack.43), channel_id=1, replica_groups=mesh['dp'=8,'tensor'=4] {'dp','tensor'}, use_global_device_ids=true, to_apply=%region_35.36 | all-reduce | flops 6912 | bytes 55296 | tf_op jit(solution)/shard_map/psum | solution.py:237
  552.2 2.9 fusion.69
  555.1 62.2 %reduce-scatter.23.cloned.1.call-done = f32[1076,144]{0,1:T(8,128)} async-done(((f32[1076,1152]{0,1:T(8,128)}), f32[1076,144]{0,1:T(8,128)}) %reduce-scatter.23.cloned.1.call-update) | async-done | bytes 619792 | tf_op jit(solution)/shard_map/reduce_scatter | solution.py:224
  617.3 108.1 %reduce-scatter.21.cloned.1.call-done = f32[144,1076]{1,0:T(8,128)} async-done(((f32[1152,1076]{1,0:T(8,128)}), f32[144,1076]{1,0:T(8,128)}) %reduce-scatter.21.cloned.1.call-update) | async-done | bytes 619792 | tf_op jit(solution)/shard_map/reduce_scatter | solution.py:223
  725.4 70.3 %reduce-scatter.19.cloned.1.call-done = f32[288,144]{0,1:T(8,128)} async-done(((f32[288,1152]{0,1:T(8,128)}), f32[288,144]{0,1:T(8,128)}) %reduce-scatter.19.cloned.1.call-update) | async-done | bytes 165904 | tf_op jit(solution)/shard_map/reduce_scatter | solution.py:222
  (203 shorter events, 21.1 us)
Async XLA Ops:
  7.2 172.5 %copy-start = (bf16[1152,1076]{0,1:T(8,128)(2,1)S(1)}, bf16[1152,1076]{0,1:T(8,128)(2,1)}, u32[]{:S(2)}) copy-start(bf16[1152,1076]{0,1:T(8,128)(2,1)} %param.29) | copy-start | bytes 7437316
  7.2 5.1 copy-start.27
  7.2 5.1 copy-start.44
  7.2 32.0 %all-gather.5.cloned.1.call-start = ((), (), s32[]{:S(2)}) async-start(), calls=%async_computation.8 | async-start | bytes 2949120 | tf_op jit(solution)/shard_map/all_gather | solution.py:63
  8.6 30.5 %copy-start.34 = (f32[256]{0:T(256)}, f32[256]{0:T(256)S(1)}, u32[]{:S(2)}) copy-start(f32[256]{0:T(256)S(1)} %broadcast_multiply_fusion.5) | copy-start | bytes 3076
  10.0 29.2 %copy-start.38 = (f32[256]{0:T(256)}, f32[256]{0:T(256)S(1)}, u32[]{:S(2)}) copy-start(f32[256]{0:T(256)S(1)} %add_rsqrt_fusion.1) | copy-start | bytes 3076
  12.2 115.5 %reduce-scatter.11.cloned.1.call-start = ((), (), s32[]{:S(2)}) async-start(), calls=%async_computation.9 | async-start | bytes 5898240 | tf_op jit(solution)/shard_map/reduce_scatter | solution.py:104
  12.4 31.6 %copy-start.36 = (f32[288]{0:T(512)}, f32[288]{0:T(512)S(1)}, u32[]{:S(2)}) copy-start(f32[288]{0:T(512)S(1)} %get-tuple-element.296) | copy-start | bytes 3460
  48.8 2.3 copy-start.13
  56.2 2.9 copy-start.5
  56.2 2.9 copy-start.16
  66.4 2.9 copy-start.5
  66.4 2.9 copy-start.16
  73.3 6.3 copy-start.45
  73.4 2.7 copy-start.22
  79.7 48.0 %copy-start.40 = (f32[1152]{0:T(1024)S(1)}, f32[1152]{0:T(1024)}, u32[]{:S(2)}) copy-start(f32[1152]{0:T(1024)} %param.26) | copy-start | bytes 13828
  79.7 50.7 %copy-start.28 = (f32[1152]{0:T(1024)S(1)}, f32[1152]{0:T(1024)}, u32[]{:S(2)}) copy-start(f32[1152]{0:T(1024)} %param.27) | copy-start | bytes 13828
  79.7 50.7 %copy-start.41 = (f32[1152]{0:T(1024)S(1)}, f32[1152]{0:T(1024)}, u32[]{:S(2)}) copy-start(f32[1152]{0:T(1024)} %param.28) | copy-start | bytes 13828
  79.7 73.7 %all-gather.9.cloned.1.call-start = ((), (), s32[]{:S(2)}) async-start(), calls=%async_computation.12 | async-start | bytes 2949120 | tf_op jit(solution)/shard_map/all_gather | solution.py:128
  80.5 99.2 %all-gather.7.cloned.1.call-start = ((), (), s32[]{:S(2)}) async-start(), calls=%async_computation.10 | async-start | bytes 2949120 | tf_op jit(solution)/shard_map/all_gather | solution.py:112
  131.5 48.1 %copy-start.48 = (f32[1076]{0:T(1024)S(1)}, f32[1076]{0:T(1024)}, u32[]{:S(2)}) copy-start(f32[1076]{0:T(1024)} %param.30) | copy-start | bytes 12916
  131.5 112.6 %reduce-scatter.15.cloned.1.call-start = ((), (), s32[]{:S(2)}) async-start(), calls=%async_computation.13 | async-start | bytes 5898240 | tf_op jit(solution)/shard_map/reduce_scatter | solution.py:134
  189.5 1.4 copy-start.50
  196.1 1.7 copy-start.47
  196.1 83.5 %reduce-scatter.13.cloned.1.call-start = ((), (), s32[]{:S(2)}) async-start(), calls=%async_computation.11 | async-start | bytes 2949120 | tf_op jit(solution)/shard_map/reduce_scatter | solution.py:115
  205.3 38.8 %copy-start.4 = (f32[256,1152]{1,0:T(8,128)S(1)}, f32[256,1152]{1,0:T(8,128)}, u32[]{:S(2)}) copy-start(f32[256,1152]{1,0:T(8,128)} %copy-done.3) | copy-start | bytes 3538948
  205.3 74.3 %copy-start.42 = (f32[1152]{0:T(1024)S(1)}, f32[1152]{0:T(1024)}, u32[]{:S(2)}) copy-start(f32[1152]{0:T(1024)} %param.32) | copy-start | bytes 13828
  205.3 103.1 %all-gather.11.cloned.1.call-start = ((), (), s32[]{:S(2)}) async-start(), calls=%async_computation.14 | async-start | bytes 2949120 | tf_op jit(solution)/shard_map/all_gather | solution.py:143
  283.2 25.2 %copy-start.8 = (f32[256,1152]{1,0:T(8,128)}, f32[256,1152]{1,0:T(8,128)S(1)}, u32[]{:S(2)}) copy-start(f32[256,1152]{1,0:T(8,128)S(1)} %get-tuple-element.340) | copy-start | bytes 3538948
  284.2 173.7 %reduce-scatter.25.cloned.1.call-start = ((), (), s32[]{:S(2)}) async-start(), calls=%async_computation.19 | async-start | bytes 4644864
  312.0 4.0 copy-start.2
  316.4 1.3 copy-start.9
  316.4 1.4 copy-start.18
  317.8 2.7 copy-start.6
  320.5 3.3 copy-start.19
  323.8 2.4 copy-start.10
  329.2 1.4 copy-start.18
  330.6 2.7 copy-start.6
  333.3 3.3 copy-start.19
  336.6 2.4 copy-start.10
  341.9 2.5 copy-start.20
  342.0 8.9 %copy-start.23 = (bf16[1024,4,72]{0,2,1:T(8,128)(2,1)}, bf16[1024,4,72]{0,2,1:T(8,128)(2,1)S(1)}, u32[]{:S(2)}) copy-start(bf16[1024,4,72]{0,2,1:T(8,128)(2,1)S(1)} %convert_element_type.109) | copy-start | bytes 1769476
  344.4 6.5 copy-start.25
  344.6 6.4 copy-start.26
  368.5 1.6 copy-start.21
  368.5 1.7 copy-start.24
  368.5 138.9 %reduce-scatter.17.cloned.1.call-start = ((), (), s32[]{:S(2)}) async-start(), calls=%async_computation.15 | async-start | bytes 5898240 | tf_op jit(solution)/shard_map/reduce_scatter | solution.py:211
  376.5 240.9 %reduce-scatter.23.cloned.1.call-start = ((), (), s32[]{:S(2)}) async-start(), calls=%async_computation.18 | async-start | bytes 5971968 | tf_op jit(solution)/shard_map/reduce_scatter | solution.py:224
  385.2 340.2 %reduce-scatter.21.cloned.1.call-start = ((), (), s32[]{:S(2)}) async-start(), calls=%async_computation.17 | async-start | bytes 5971968 | tf_op jit(solution)/shard_map/reduce_scatter | solution.py:223
  393.4 5.6 copy-start.46
  393.5 27.8 %copy-start.37 = (f32[288]{0:T(512)S(1)}, f32[288]{0:T(512)}, u32[]{:S(2)}) copy-start(f32[288]{0:T(512)} %copy-done.36) | copy-start | bytes 3460
  393.5 402.3 %reduce-scatter.19.cloned.1.call-start = ((), (), s32[]{:S(2)}) async-start(), calls=%async_computation.16 | async-start | bytes 1990656 | tf_op jit(solution)/shard_map/reduce_scatter | solution.py:222
  399.0 24.2 %copy-start.31 = (f32[1152]{0:T(1024)S(1)}, f32[1152]{0:T(1024)}, u32[]{:S(2)}) copy-start(f32[1152]{0:T(1024)} %get-tuple-element.287) | copy-start | bytes 13828
  399.0 24.2 %copy-start.33 = (f32[1152]{0:T(1024)S(1)}, f32[1152]{0:T(1024)}, u32[]{:S(2)}) copy-start(f32[1152]{0:T(1024)} %get-tuple-element.339) | copy-start | bytes 13828
  399.0 24.2 %copy-start.32 = (f32[1152]{0:T(1024)S(1)}, f32[1152]{0:T(1024)}, u32[]{:S(2)}) copy-start(f32[1152]{0:T(1024)} %get-tuple-element.354) | copy-start | bytes 13828
  399.0 24.3 %copy-start.30 = (f32[1152]{0:T(1024)S(1)}, f32[1152]{0:T(1024)}, u32[]{:S(2)}) copy-start(f32[1152]{0:T(1024)} %get-tuple-element.293) | copy-start | bytes 13828
  399.0 24.3 %copy-start.12 = (bf16[2,512,4,72]{1,3,2,0:T(8,128)(2,1)S(1)}, bf16[2,512,4,72]{1,3,2,0:T(8,128)(2,1)}, u32[]{:S(2)}) copy-start(bf16[2,512,4,72]{1,3,2,0:T(8,128)(2,1)} %get-tuple-element.176) | copy-start | bytes 1769476
  399.0 24.6 %copy-start.43 = (f32[1076]{0:T(1024)S(1)}, f32[1076]{0:T(1024)}, u32[]{:S(2)}) copy-start(f32[1076]{0:T(1024)} %get-tuple-element.341) | copy-start | bytes 12916
  421.1 39.2 %copy-start.49 = (f32[4]{0:T(128)}, f32[4]{0:T(128)S(1)}, u32[]{:S(2)}) copy-start(f32[4]{0:T(128)S(1)} %pmax.7) | copy-start | bytes 52
  423.2 84.2 %copy-start.7 = (bf16[256,1152]{1,0:T(8,128)(2,1)S(1)}, bf16[256,1152]{1,0:T(8,128)(2,1)}, u32[]{:S(2)}) copy-start(bf16[256,1152]{1,0:T(8,128)(2,1)} %param.19) | copy-start | bytes 1769476
  423.2 84.2 %copy-start.29 = (f32[1152]{0:T(1024)S(1)}, f32[1152]{0:T(1024)}, u32[]{:S(2)}) copy-start(f32[1152]{0:T(1024)} %param.21) | copy-start | bytes 13828
  423.2 84.2 %copy-start.35 = (f32[256]{0:T(256)S(1)}, f32[256]{0:T(256)}, u32[]{:S(2)}) copy-start(f32[256]{0:T(256)} %copy-done.34) | copy-start | bytes 3076
  423.2 84.2 %copy-start.39 = (f32[256]{0:T(256)S(1)}, f32[256]{0:T(256)}, u32[]{:S(2)}) copy-start(f32[256]{0:T(256)} %copy-done.38) | copy-start | bytes 3076
  460.3 335.5 %copy-start.1 = (bf16[1152,1076]{0,1:T(8,128)(2,1)S(1)}, bf16[1152,1076]{0,1:T(8,128)(2,1)}, u32[]{:S(2)}) copy-start(bf16[1152,1076]{0,1:T(8,128)(2,1)} %param.29) | copy-start | bytes 7437316
  (8 other events, 8.0 us)
Sparse Core Ops, SparseCore 0:
  12.4 26.7 all-gather.4
  79.8 47.8 reduce-scatter.10
  129.4 24.0 all-gather.8
  155.5 24.0 all-gather.6
  196.2 47.8 reduce-scatter.14
  246.5 33.0 reduce-scatter.12
  284.3 24.0 all-gather.10
  368.6 88.3 reduce-scatter.24
  459.6 47.7 reduce-scatter.16
  511.8 105.4 reduce-scatter.22
  621.5 103.8 reduce-scatter.20
  729.7 65.9 reduce-scatter.18
where the time goes:
time: 812 us; the launch traced here: 803 us
  waiting for transfers between devices  496 us (61%)
  matrix products  107 us (13%)
  blocking collectives  99.1 us (12%)
  local copies, waits for them, and re-layouts  46 us (6%)
  other arithmetic  37.6 us (5%)
  between operations  14.9 us (2%)
    reduce_scatter x1, waiting for transfers between devices, local(): lax.psum_scatter(grad_up, 'dp', scatter_dimension=0, tiled=True)  108 us
    reduce_scatter x1, waiting for transfers between devices, local(): lax.psum_scatter(grad_out, 'dp', scatter_dimension=1, tiled=True)  70.3 us
    reduce_scatter x1, waiting for transfers between devices, local(): lax.psum_scatter(grad_down, 'dp', scatter_dimension=1, tiled=True)  62.2 us
    reduce_scatter x1, waiting for transfers between devices, local(): lax.psum_scatter(jnp.dot(flat_att, w_out, preferred_element_type=jnp.floa...  47.2 us
    reduce_scatter x1, waiting for transfers between devices, local(): lax.psum_scatter(jnp.einsum('cte,cde->td', grad_stack, w_qkv, preferred_e...  44.9 us
    psum x1, blocking collectives, local(): grad_shared = lax.psum(shared_part, ('dp', 'tensor'))  42.9 us
    reduce_scatter x1, waiting for transfers between devices, local(): lax.psum_scatter(jnp.einsum('tf,df->td', grad_pre, w_up, preferred_elemen...  38.8 us
    psum x1, blocking collectives, local(): grad_qv_bias, grad_up_bias = lax.psum((grad_qv_bias, grad_up_bias), 'dp')  34.2 us
  transfers between devices with their start and end apart: 12, of which 11 were waited for; matrix products, arithmetic and copies ran while one was open for 7% of the time, Pallas kernels for 0%

commit v1 on v0

--- a/solution.py
+++ b/solution.py
@@ -109,7 +109,24 @@
     )
     residual = source + branch_a + out_bias
     normed_b, unit_b, inverse_b = normalize(residual, norm2_gain, norm2_bias)
-    whole_b = lax.all_gather(normed_b.astype(jnp.bfloat16), "tensor", axis=0, tiled=True)
+    shard = normed_b.astype(jnp.bfloat16)
+    length, index, rows = (lax.axis_size("tensor"), lax.axis_index("tensor"), shard.shape[0])
+    right = [(i, (i + 1) % length) for i in range(length)]
+    left = [(i, (i - 1) % length) for i in range(length)]
+    whole_b = jnp.zeros((*shard.shape[:0], length * rows, *shard.shape[0 + 1 :]), shard.dtype)
+    whole_b = lax.dynamic_update_slice_in_dim(whole_b, shard, index * rows, axis=0)
+    from_left = from_right = shard
+    half = length // 2
+    for step in range(1, half + 1):
+        from_left = lax.ppermute(from_left, "tensor", right)
+        whole_b = lax.dynamic_update_slice_in_dim(
+            whole_b, from_left, (index - step) % length * rows, axis=0
+        )
+        if step < length - half:
+            from_right = lax.ppermute(from_right, "tensor", left)
+            whole_b = lax.dynamic_update_slice_in_dim(
+                whole_b, from_right, (index + step) % length * rows, axis=0
+            )
     pre_act = jnp.dot(whole_b, w_up, preferred_element_type=jnp.float32) + up_bias
     activated = gelu_tanh(pre_act).astype(jnp.bfloat16)
     branch_b = lax.psum_scatter(

time: 812 us -> 804 us (level)
  waiting for transfers between devices: 496 us -> 485 us
    ppermute x0 -> x3, waiting for transfers between devices: none -> 22.4 us  [the longest x2 22.4 us: local(): from_left = lax.ppermute(from_left, 'tensor', right)]
    all_gather x1 -> x0, waiting for transfers between devices: 18.6 us -> none  [local(): lax.all_gather(normed_b.astype(jnp.bfloat16), 'tensor', axis=0, tiled=True)]
    all_gather x1, waiting for transfers between devices: 21.7 us -> 6.45 us  [local(): whole_grad = lax.all_gather(cotangent, 'tensor', axis=0, tiled=True)]
    unnamed x90 -> x98, local copies, waits for them, and re-layouts: 30.4 us -> 34.3 us
  transfers between devices with their start and end apart: 12 -> 14, of which waited for: 11 -> 11; matrix products, arithmetic and copies ran while one was open for 7% -> 7% of each run, Pallas kernels for 0% -> 0%
where the time goes in v1:
time: 804 us; the launch traced here: 794 us
  waiting for transfers between devices  485 us (60%)
  matrix products  102 us (13%)
  blocking collectives  98.5 us (12%)
  local copies, waits for them, and re-layouts  53.3 us (7%)
  other arithmetic  37.6 us (5%)
  between operations  14.7 us (2%)
    reduce_scatter x1, waiting for transfers between devices, local(): lax.psum_scatter(grad_up, 'dp', scatter_dimension=0, tiled=True)  108 us
    reduce_scatter x1, waiting for transfers between devices, local(): lax.psum_scatter(grad_out, 'dp', scatter_dimension=1, tiled=True)  70.8 us
    reduce_scatter x1, waiting for transfers between devices, local(): lax.psum_scatter(grad_down, 'dp', scatter_dimension=1, tiled=True)  62.1 us
    reduce_scatter x1, waiting for transfers between devices, local(): lax.psum_scatter(jnp.dot(flat_att, w_out, preferred_element_type=jnp.floa...  47.2 us
    reduce_scatter x1, waiting for transfers between devices, local(): lax.psum_scatter(jnp.einsum('cte,cde->td', grad_stack, w_qkv, preferred_e...  43.8 us
    psum x1, blocking collectives, local(): grad_shared = lax.psum(shared_part, ('dp', 'tensor'))  42.9 us
    reduce_scatter x1, waiting for transfers between devices, local(): lax.psum_scatter(jnp.einsum('tf,df->td', grad_pre, w_up, preferred_elemen...  39.7 us
    unnamed x98, local copies, waits for them, and re-layouts  34.3 us
  transfers between devices with their start and end apart: 14, of which 11 were waited for; matrix products, arithmetic and copies ran while one was open for 7% of the time, Pallas kernels for 0%

profile of v1, /device:TPU:0, one launch (start us, length us, event | category | flops | bytes accessed | tf_op | source)
XLA Modules:
  0.0 794.4 jit_solution(15693201338768473282)
XLA Ops:
  10.0 2.2 fusion.64
  12.5 26.6 %all-gather.4.cloned.1.call-done = bf16[1024,1152]{1,0:T(8,128)(2,1)} async-done(((bf16[256,1152]{1,0:T(8,128)(2,1)}), bf16[1024,1152]{1,0:T(8,128)(2,1)}) %all-gather.4.cloned.1.call-update) | async-done | bytes 2359312 | tf_op jit(solution)/shard_map/all_gather | solution.py:63
  39.2 4.7 fusion.54
  44.0 1.6 fusion.81
  45.6 3.2 squeeze.52
  48.8 2.3 add_convert_fusion.2
  53.0 20.3 %while.51 = (s32[]{:T(128)}, bf16[2,512,4,72]{1,3,2,0:T(8,128)(2,1)}, f32[2,4,512]{2,1,0:T(4,128)S(1)}, f32[2,4]{1,0:T(2,128)S(1)}, s32[2,512]{1,0:T(2,128)S(1)}...) while((s32[]{:T(128)}, ...), condition=%wide.region_6.7_spmd, body=%wide.region_2.6_spmd.sunk | while | flops 631912448 | bytes 36186380 | solution.py:98
  53.4 2.8 fusion.132
  56.2 2.9 fusion.133
  59.2 3.1 fusion.134
  63.6 2.8 fusion.132
  66.4 2.9 fusion.133
  69.4 3.1 fusion.134
  73.4 1.7 copy.37
  76.1 3.6 fusion.82
  80.5 47.2 %reduce-scatter.11.cloned.1.call-done = f32[256,1152]{1,0:T(8,128)} async-done(((f32[1024,1152]{1,0:T(8,128)}), f32[256,1152]{1,0:T(8,128)}) %reduce-scatter.11.cloned.1.call-update) | async-done | bytes 1179664 | tf_op jit(solution)/shard_map/reduce_scatter | solution.py:104
  127.7 1.7 fusion.79
  131.3 1.4 copy-done.16
  133.0 1.7 collective-permute-start.1
  134.7 22.4 %collective-permute-done = bf16[256,1152]{1,0:T(8,128)(2,1)} collective-permute-done((bf16[256,1152]{1,0:T(8,128)(2,1)}, bf16[256,1152]{1,0:T(8,128)(2,1)}, u32[]{:S(2)}, u32[]{:S(2)}) %collective-permute-start) | collective-permute-done | bytes 589856 | tf_op jit(solution)/shard_map/ppermute | solution.py:121
  157.1 6.5 all-gather.6.cloned.1.call-done
  163.5 5.6 fusion.83
  172.7 7.8 convert_reduce_fusion
  181.9 5.2 fusion.84
  187.1 1.6 copy-done.50
  188.8 7.4 convolution_convert_fusion
  196.3 39.7 %reduce-scatter.15.cloned.1.call-done = f32[256,1152]{1,0:T(8,128)} async-done(((f32[1024,1152]{1,0:T(8,128)}), f32[256,1152]{1,0:T(8,128)}) %reduce-scatter.15.cloned.1.call-update) | async-done | bytes 1179664 | tf_op jit(solution)/shard_map/reduce_scatter | solution.py:151
  236.0 2.4 multiply_reduce_fusion.1
  238.4 33.1 %reduce-scatter.13.cloned.1.call-done = bf16[256,1152]{1,0:T(8,128)(2,1)} async-done(((bf16[1024,1152]{1,0:T(8,128)(2,1)}), bf16[256,1152]{1,0:T(8,128)(2,1)}) %reduce-scatter.13.cloned.1.call-update) | async-done | bytes 589840 | tf_op jit(solution)/shard_map/reduce_scatter | solution.py:132
  271.5 3.6 fusion.77
  276.4 23.9 %all-gather.8.cloned.1.call-done = bf16[1024,1152]{1,0:T(8,128)(2,1)} async-done(((bf16[256,1152]{1,0:T(8,128)(2,1)}), bf16[1024,1152]{1,0:T(8,128)(2,1)}) %all-gather.8.cloned.1.call-update) | async-done | bytes 2359312 | tf_op jit(solution)/shard_map/all_gather | solution.py:160
  300.3 3.6 convolution_convert_fusion.1
  303.9 2.3 squeeze.54
  307.9 25.9 %while.52 = (s32[]{:T(128)}, f32[1024,4,72]{0,2,1:T(8,128)S(1)}, f32[1024,4,72]{0,2,1:T(8,128)}, bf16[2,512,4,72]{1,3,2,0:T(8,128)(2,1)}, bf16[2,512,4,72]{1,3,2...) while((s32[]{:T(128)}, f32[1024,4,72]{0,2,1:T(8,128)S(1)}, ...), condition=%wide.region_16.17_spmd.clone, body=%wide.region_14.16_spmd.clone.sunk | while | flops 1543698432 | bytes 91916632 | solution.py:205
  309.8 2.6 fusion.146
  312.4 3.3 multiply_reduce_fusion.7
  315.7 2.4 multiply_convert_fusion.6
  318.2 1.4 fusion.147
  322.5 2.6 fusion.146
  325.2 3.3 multiply_reduce_fusion.7
  328.5 2.4 multiply_convert_fusion.6
  330.9 1.4 fusion.147
  333.9 1.8 copy.39
  336.3 6.4 convolution_bitcast_fusion.1
  342.6 8.6 %copy.41 = f32[3,1152,288]{2,0,1:T(4,128)} copy(f32[3,1152,288]{1,2,0:T(8,128)} %convolution_bitcast_fusion.1) | data formatting | bytes 7962624
  351.2 8.9 %reshape.211 = f32[1152,864]{1,0:T(8,128)} reshape(f32[1152,3,288]{2,1,0:T(4,128)} %bitcast.143) | data formatting | bytes 7962624
  360.2 1.5 copy-done.25
  361.7 6.3 convolution_bitcast_fusion
  368.1 1.6 copy-done.51
  369.7 7.9 fusion.76
  377.8 1.5 copy-done.19
  379.3 7.3 fusion.86
  387.7 4.6 fusion.85
  392.4 21.8 %pmax.7 = f32[4]{0:T(128)S(1)} all-reduce(f32[4]{0:T(128)S(1)} %reduce_max.27), channel_id=1, replica_groups=mesh['dp'=8,'tensor'=4] {'dp'}, use_global_device_ids=true, to_apply=%region_37.38 | all-reduce | flops 4 | bytes 32 | tf_op jit(solution)/shard_map/pmax | solution.py:139
  416.8 33.8 %all-reduce = (f32[2,288]{1,0:T(2,128)}, f32[1076]{0:T(1024)}) all-reduce(f32[2,288]{1,0:T(2,128)S(1)} %pad_maximum_fusion.3, f32[1076]{0:T(1024)S(1)} %copy-done.46), channel_id=1, replica_groups=mesh['dp'=8,'tensor'=4] {'dp'}, use_global_device_ids=true, to_apply=%region_26.27 | all-reduce | flops 1652 | bytes 13216 | tf_op jit(solution)/shard_map/psum | solution.py:243
  450.5 2.4 reshape.212
  452.9 2.2 copy.40
  455.1 43.8 %reduce-scatter.17.cloned.1.call-done = f32[256,1152]{1,0:T(8,128)} async-done(((f32[1024,1152]{1,0:T(8,128)}), f32[256,1152]{1,0:T(8,128)}) %reduce-scatter.17.cloned.1.call-update) | async-done | bytes 1179664 | tf_op jit(solution)/shard_map/reduce_scatter | solution.py:228
  499.0 1.9 fusion.70
  500.9 42.9 %psum.23 = f32[6,1152]{1,0:T(8,128)} all-reduce(f32[6,1152]{1,0:T(8,128)S(1)} %stack.43), channel_id=1, replica_groups=mesh['dp'=8,'tensor'=4] {'dp','tensor'}, use_global_device_ids=true, to_apply=%region_35.36 | all-reduce | flops 6912 | bytes 55296 | tf_op jit(solution)/shard_map/psum | solution.py:254
  543.9 2.9 fusion.69
  546.8 62.1 %reduce-scatter.23.cloned.1.call-done = f32[1076,144]{0,1:T(8,128)} async-done(((f32[1076,1152]{0,1:T(8,128)}), f32[1076,144]{0,1:T(8,128)}) %reduce-scatter.23.cloned.1.call-update) | async-done | bytes 619792 | tf_op jit(solution)/shard_map/reduce_scatter | solution.py:241
  608.8 108.0 %reduce-scatter.21.cloned.1.call-done = f32[144,1076]{1,0:T(8,128)} async-done(((f32[1152,1076]{1,0:T(8,128)}), f32[144,1076]{1,0:T(8,128)}) %reduce-scatter.21.cloned.1.call-update) | async-done | bytes 619792 | tf_op jit(solution)/shard_map/reduce_scatter | solution.py:240
  716.9 70.8 %reduce-scatter.19.cloned.1.call-done = f32[288,144]{0,1:T(8,128)} async-done(((f32[288,1152]{0,1:T(8,128)}), f32[288,144]{0,1:T(8,128)}) %reduce-scatter.19.cloned.1.call-update) | async-done | bytes 165904 | tf_op jit(solution)/shard_map/reduce_scatter | solution.py:239
  (218 shorter events, 29.7 us)
Async XLA Ops:
  7.2 165.5 %copy-start = (bf16[1152,1076]{0,1:T(8,128)(2,1)S(1)}, bf16[1152,1076]{0,1:T(8,128)(2,1)}, u32[]{:S(2)}) copy-start(bf16[1152,1076]{0,1:T(8,128)(2,1)} %param.29) | copy-start | bytes 7437316
  7.2 5.1 copy-start.30
  7.2 5.1 copy-start.47
  7.2 32.0 %all-gather.4.cloned.1.call-start = ((), (), s32[]{:S(2)}) async-start(), calls=%async_computation.8 | async-start | bytes 2949120 | tf_op jit(solution)/shard_map/all_gather | solution.py:63
  8.6 30.5 %copy-start.37 = (f32[256]{0:T(256)}, f32[256]{0:T(256)S(1)}, u32[]{:S(2)}) copy-start(f32[256]{0:T(256)S(1)} %broadcast_multiply_fusion.5) | copy-start | bytes 3076
  10.0 29.2 %copy-start.41 = (f32[256]{0:T(256)}, f32[256]{0:T(256)S(1)}, u32[]{:S(2)}) copy-start(f32[256]{0:T(256)S(1)} %add_rsqrt_fusion.1) | copy-start | bytes 3076
  12.2 115.5 %reduce-scatter.11.cloned.1.call-start = ((), (), s32[]{:S(2)}) async-start(), calls=%async_computation.9 | async-start | bytes 5898240 | tf_op jit(solution)/shard_map/reduce_scatter | solution.py:104
  12.4 31.6 %copy-start.39 = (f32[288]{0:T(512)}, f32[288]{0:T(512)S(1)}, u32[]{:S(2)}) copy-start(f32[288]{0:T(512)S(1)} %get-tuple-element.296) | copy-start | bytes 3460
  48.8 2.3 copy-start.13
  56.2 2.9 copy-start.5
  56.2 2.9 copy-start.20
  66.4 2.9 copy-start.5
  66.4 2.9 copy-start.20
  73.4 6.3 copy-start.48
  73.4 2.7 copy-start.27
  79.7 48.0 %copy-start.43 = (f32[1152]{0:T(1024)S(1)}, f32[1152]{0:T(1024)}, u32[]{:S(2)}) copy-start(f32[1152]{0:T(1024)} %param.26) | copy-start | bytes 13828
  79.7 83.8 %all-gather.6.cloned.1.call-start = ((), (), s32[]{:S(2)}) async-start(), calls=%async_computation.11 | async-start | bytes 2949120 | tf_op jit(solution)/shard_map/all_gather | solution.py:145
  80.5 155.6 %reduce-scatter.15.cloned.1.call-start = ((), (), s32[]{:S(2)}) async-start(), calls=%async_computation.12 | async-start | bytes 5898240 | tf_op jit(solution)/shard_map/reduce_scatter | solution.py:151
  129.4 2.0 copy-start.3
  132.8 24.3 %collective-permute-start = (bf16[256,1152]{1,0:T(8,128)(2,1)}, bf16[256,1152]{1,0:T(8,128)(2,1)}, u32[]{:S(2)}, u32[]{:S(2)}) collective-permute-start(bf16[256,1152]{1,0:T(8,128)(2,1)} %get-tuple-element.346), channel_id=1, source_target_pairs={{0,1},{1,2},{2,3},{3,0},{4,5},{5,6},{6,7},{7,4},{8,9},{9,10},{10,1... | collective-permute-start | bytes 1769480 | tf_op jit(solution)/shard_map/ppermute | solution.py:121
  133.0 37.3 %collective-permute-start.1 = (bf16[256,1152]{1,0:T(8,128)(2,1)}, bf16[256,1152]{1,0:T(8,128)(2,1)}, u32[]{:S(2)}, u32[]{:S(2)}) collective-permute-start(bf16[256,1152]{1,0:T(8,128)(2,1)} %get-tuple-element.346), channel_id=1, source_target_pairs={{0,3},{1,0},{2,1},{3,2},{4,7},{5,4},{6,5},{7,6},{8,11},{9,8},{10,9... | collective-permute-start | bytes 1769480 | tf_op jit(solution)/shard_map/ppermute | solution.py:126
  157.1 14.4 %collective-permute-start.2 = (bf16[256,1152]{1,0:T(8,128)(2,1)}, bf16[256,1152]{1,0:T(8,128)(2,1)}, u32[]{:S(2)}, u32[]{:S(2)}) collective-permute-start(bf16[256,1152]{1,0:T(8,128)(2,1)} %collective-permute-done), channel_id=1, source_target_pairs={{0,1},{1,2},{2,3},{3,0},{4,5},{5,6},{6,7},{7,4},{8,9},{9,10},{10,1... | collective-permute-start | bytes 1769480 | tf_op jit(solution)/shard_map/ppermute | solution.py:121
  163.5 5.7 copy-start.17
  169.2 3.5 copy-start.52
  172.7 7.8 copy-start.18
  187.1 1.7 copy-start.50
  187.1 84.4 %reduce-scatter.13.cloned.1.call-start = ((), (), s32[]{:S(2)}) async-start(), calls=%async_computation.10 | async-start | bytes 2949120 | tf_op jit(solution)/shard_map/reduce_scatter | solution.py:132
  196.2 39.8 %copy-start.4 = (f32[256,1152]{1,0:T(8,128)S(1)}, f32[256,1152]{1,0:T(8,128)}, u32[]{:S(2)}) copy-start(f32[256,1152]{1,0:T(8,128)} %copy-done.3) | copy-start | bytes 3538948
  196.2 75.3 %copy-start.45 = (f32[1152]{0:T(1024)S(1)}, f32[1152]{0:T(1024)}, u32[]{:S(2)}) copy-start(f32[1152]{0:T(1024)} %param.32) | copy-start | bytes 13828
  196.2 104.1 %all-gather.8.cloned.1.call-start = ((), (), s32[]{:S(2)}) async-start(), calls=%async_computation.13 | async-start | bytes 2949120 | tf_op jit(solution)/shard_map/all_gather | solution.py:160
  275.1 25.2 %copy-start.8 = (f32[256,1152]{1,0:T(8,128)}, f32[256,1152]{1,0:T(8,128)S(1)}, u32[]{:S(2)}) copy-start(f32[256,1152]{1,0:T(8,128)S(1)} %get-tuple-element.340) | copy-start | bytes 3538948
  276.1 174.4 %reduce-scatter.25.cloned.1.call-start = ((), (), s32[]{:S(2)}) async-start(), calls=%async_computation.18 | async-start | bytes 4644864
  303.9 4.0 copy-start.2
  309.8 2.7 copy-start.6
  312.4 3.3 copy-start.23
  315.7 2.4 copy-start.10
  322.5 2.7 copy-start.6
  325.2 3.3 copy-start.23
  328.5 2.4 copy-start.10
  333.8 2.3 copy-start.24
  336.1 6.6 copy-start.28
  336.3 6.4 copy-start.29
  360.1 1.6 copy-start.25
  360.2 138.8 %reduce-scatter.17.cloned.1.call-start = ((), (), s32[]{:S(2)}) async-start(), calls=%async_computation.14 | async-start | bytes 5898240 | tf_op jit(solution)/shard_map/reduce_scatter | solution.py:228
  368.0 1.7 copy-start.51
  368.1 240.8 %reduce-scatter.23.cloned.1.call-start = ((), (), s32[]{:S(2)}) async-start(), calls=%async_computation.17 | async-start | bytes 5971968 | tf_op jit(solution)/shard_map/reduce_scatter | solution.py:241
  377.6 1.7 copy-start.19
  377.6 339.3 %reduce-scatter.21.cloned.1.call-start = ((), (), s32[]{:S(2)}) async-start(), calls=%async_computation.16 | async-start | bytes 5971968 | tf_op jit(solution)/shard_map/reduce_scatter | solution.py:240
  386.6 5.7 copy-start.49
  386.6 27.7 %copy-start.40 = (f32[288]{0:T(512)S(1)}, f32[288]{0:T(512)}, u32[]{:S(2)}) copy-start(f32[288]{0:T(512)} %copy-done.39) | copy-start | bytes 3460
  386.6 401.0 %reduce-scatter.19.cloned.1.call-start = ((), (), s32[]{:S(2)}) async-start(), calls=%async_computation.15 | async-start | bytes 1990656 | tf_op jit(solution)/shard_map/reduce_scatter | solution.py:239
  387.7 27.2 %copy-start.26 = (bf16[3,1152,288]{1,2,0:T(8,128)(2,1)S(1)}, bf16[3,1152,288]{1,2,0:T(8,128)(2,1)}, u32[]{:S(2)}) copy-start(bf16[3,1152,288]{1,2,0:T(8,128)(2,1)} %param.23) | copy-start | bytes 5971972
  392.3 24.0 %copy-start.34 = (f32[1152]{0:T(1024)S(1)}, f32[1152]{0:T(1024)}, u32[]{:S(2)}) copy-start(f32[1152]{0:T(1024)} %get-tuple-element.287) | copy-start | bytes 13828
  392.3 24.0 %copy-start.36 = (f32[1152]{0:T(1024)S(1)}, f32[1152]{0:T(1024)}, u32[]{:S(2)}) copy-start(f32[1152]{0:T(1024)} %get-tuple-element.339) | copy-start | bytes 13828
  392.3 24.1 %copy-start.35 = (f32[1152]{0:T(1024)S(1)}, f32[1152]{0:T(1024)}, u32[]{:S(2)}) copy-start(f32[1152]{0:T(1024)} %get-tuple-element.356) | copy-start | bytes 13828
  392.3 24.1 %copy-start.33 = (f32[1152]{0:T(1024)S(1)}, f32[1152]{0:T(1024)}, u32[]{:S(2)}) copy-start(f32[1152]{0:T(1024)} %get-tuple-element.293) | copy-start | bytes 13828
  392.3 24.1 %copy-start.12 = (bf16[2,512,4,72]{1,3,2,0:T(8,128)(2,1)S(1)}, bf16[2,512,4,72]{1,3,2,0:T(8,128)(2,1)}, u32[]{:S(2)}) copy-start(bf16[2,512,4,72]{1,3,2,0:T(8,128)(2,1)} %get-tuple-element.176) | copy-start | bytes 1769476
  392.3 24.5 %copy-start.46 = (f32[1076]{0:T(1024)S(1)}, f32[1076]{0:T(1024)}, u32[]{:S(2)}) copy-start(f32[1076]{0:T(1024)} %get-tuple-element.341) | copy-start | bytes 12916
  414.2 38.8 %copy-start.53 = (f32[4]{0:T(128)}, f32[4]{0:T(128)S(1)}, u32[]{:S(2)}) copy-start(f32[4]{0:T(128)S(1)} %pmax.7) | copy-start | bytes 52
  416.3 82.7 %copy-start.7 = (bf16[256,1152]{1,0:T(8,128)(2,1)S(1)}, bf16[256,1152]{1,0:T(8,128)(2,1)}, u32[]{:S(2)}) copy-start(bf16[256,1152]{1,0:T(8,128)(2,1)} %param.19) | copy-start | bytes 1769476
  416.3 82.7 %copy-start.32 = (f32[1152]{0:T(1024)S(1)}, f32[1152]{0:T(1024)}, u32[]{:S(2)}) copy-start(f32[1152]{0:T(1024)} %param.21) | copy-start | bytes 13828
  416.3 82.7 %copy-start.38 = (f32[256]{0:T(256)S(1)}, f32[256]{0:T(256)}, u32[]{:S(2)}) copy-start(f32[256]{0:T(256)} %copy-done.37) | copy-start | bytes 3076
  416.3 82.7 %copy-start.42 = (f32[256]{0:T(256)S(1)}, f32[256]{0:T(256)}, u32[]{:S(2)}) copy-start(f32[256]{0:T(256)} %copy-done.41) | copy-start | bytes 3076
  452.9 334.7 %copy-start.1 = (bf16[1152,1076]{0,1:T(8,128)(2,1)S(1)}, bf16[1152,1076]{0,1:T(8,128)(2,1)}, u32[]{:S(2)}) copy-start(bf16[1152,1076]{0,1:T(8,128)(2,1)} %param.29) | copy-start | bytes 7437316
  (14 other events, 15.5 us)
Sparse Core Ops, SparseCore 0:
  12.4 26.7 all-gather.3
  79.8 47.8 reduce-scatter.10
  129.4 34.1 all-gather.5
  187.2 48.7 reduce-scatter.14
  238.4 33.0 reduce-scatter.12
  276.2 24.0 all-gather.7
  360.3 88.3 reduce-scatter.24
  451.2 47.6 reduce-scatter.16
  503.6 105.2 reduce-scatter.22
  612.9 103.9 reduce-scatter.20
  721.3 66.2 reduce-scatter.18
